TPU v7x, 256 devices: a whole 4x4x8 slice. The times are simulated.
256 devices in a mesh: dp: 64 (over x, z, core), outer: 4 (over y).
Axes of the slice: x: 4, y: 4, z: 8, core: 2. Of those that a mesh axis runs over, the one named last changes fastest.
Arguments:
- gradients: bfloat16 [64, 4, 2, 1024, 896], P('dp', 'outer'), may hold values from -48 to 48
- errors: bfloat16 [64, 4, 2, 1024, 896], P('dp', 'outer'), may hold values from -3 to 3
- old_basis: float32 [2, 896, 8], replicated, may hold values from -4 to 4
Outputs:
- new_errors: bfloat16 [64, 4, 2, 1024, 896], P('dp', 'outer')
- new_basis: float32 [2, 896, 8], replicated
All inputs are finite; a program needn't handle non-finite values.
Results may differ from a plain program's by a relative error of at most 0.001.
Values sent between devices are 32-bit elements; how exact they have to be, the bound alone decides.
A program may use at most 64 MiB of HBM per device.

v0:
```python
import jax
import jax.numpy as jnp
from jax import lax
from jax.sharding import PartitionSpec as P

HIGHEST = lax.Precision.HIGHEST
EPSILON = 1e-06


def sum_left(partial_left):
    group_sum = lax.psum(partial_left, "dp")
    return lax.psum(group_sum, "outer")


def sum_right(partial_right):
    group_sum = lax.psum(partial_right, "dp")
    return lax.psum(group_sum, "outer")


def solve_lower(lower_factor, target):
    solved = jax.vmap(
        lambda factor, values: jax.scipy.linalg.solve_triangular(factor, values, lower=True)
    )(lower_factor, jnp.swapaxes(target, 1, 2))
    return jnp.swapaxes(solved, 1, 2)


def compress(grad_part, error_part, basis_part, replicas):
    merged = grad_part.astype(jnp.float32) + error_part.astype(jnp.float32)
    partial_left = jnp.einsum("krc,kcs->krs", merged, basis_part, precision=HIGHEST)
    left_mean = sum_left(partial_left) / replicas
    rank_size = basis_part.shape[2]
    gram_matrix = jnp.einsum("krs,krt->kst", left_mean, left_mean, precision=HIGHEST)
    gram_matrix = gram_matrix + EPSILON * jnp.eye(rank_size, dtype=jnp.float32)
    lower_factor = jnp.linalg.cholesky(gram_matrix)
    orthonormal = solve_lower(lower_factor, left_mean)
    partial_right = jnp.einsum("krc,krs->kcs", merged, orthonormal, precision=HIGHEST)
    new_basis = sum_right(partial_right) / replicas
    update = jnp.einsum("krs,kcs->krc", orthonormal, new_basis, precision=HIGHEST)
    return ((merged - update).astype(jnp.bfloat16), new_basis)


def shards(gradients, errors, old_basis):
    grad_local = gradients[0, 0]
    error_local = errors[0, 0]
    replicas = lax.axis_size("dp") * lax.axis_size("outer")
    pieces = [
        compress(
            grad_local[member : member + 1],
            error_local[member : member + 1],
            old_basis[member : member + 1],
            replicas,
        )
        for member in range(grad_local.shape[0])
    ]
    residual = jnp.concatenate([piece[0] for piece in pieces], axis=0)
    new_basis = jnp.concatenate([piece[1] for piece in pieces], axis=0)
    return (residual[None, None], new_basis)


def solution(mesh):
    in_specs = (P("dp", "outer", None, None, None), P("dp", "outer", None, None, None), P())
    out_specs = (P("dp", "outer", None, None, None), P())
    return jax.shard_map(shards, mesh=mesh, in_specs=in_specs, out_specs=out_specs, check_vma=False)
```

profile of v0, /device:TPU:0, one launch (start us, length us, event | category | flops | bytes accessed | tf_op | source)
XLA Modules:
  0.0 537.0 jit_solution(8338454211307368301)
XLA Ops:
  7.2 6.3 %fusion.23 = f32[1,1024,8]{1,2,0:T(8,128)} fusion(bf16[1,1,2,1024,896]{4,3,2,1,0:T(8,128)(2,1)} %param.7, bf16[1,1,2,1024,896]{4,3,2,1,0:T(8,128)(2,1)} %param.6, f32[2,896,8]{1,2,0:T(8,128)} %param.8), kind=kOutput, calls=%fused_computation.26 | convolution fusion | flops 90832896 | bytes 3731456 | tf_op jit(solution)/shard_map/krc,kcs->krs/dot_general | solution.py:29
  13.5 5.6 %fusion.20 = f32[1,1024,8]{1,2,0:T(8,128)} fusion(bf16[1,1,2,1024,896]{4,3,2,1,0:T(8,128)(2,1)S(1)} %copy-done, bf16[1,1,2,1024,896]{4,3,2,1,0:T(8,128)(2,1)} %param.6, f32[2,896,8]{1,2,0:T(8,128)S(1)} %copy-done.3), kind=kOutput, calls=%fused_computation.25 | convolution fusion | flops 90832896 | bytes 3731456 | tf_op jit(solution)/shard_map/krc,kcs->krs/dot_general | solution.py:29
  19.2 169.3 %all-reduce.7.cloned.1.call-done = (f32[1,1024,8]{1,2,0:T(8,128)}, f32[1,1024,8]{1,2,0:T(8,128)}) async-done(((f32[1,1024,8]{1,2,0:T(8,128)}, f32[1,1024,8]{1,2,0:T(8,128)}), (f32[1,1024,8]{1,2,0:T(8,128)}, f32[1,1024,8]{1,2,0:T(8,128)})) %all-reduce.7.cloned.1.call-update) | async-done | bytes 65552 | tf_op jit(solution)/shard_map/psum | solution.py:11
  188.6 45.5 %all-reduce.9.cloned.1.call-done = (f32[1,1024,8]{1,2,0:T(8,128)}, f32[1,1024,8]{1,2,0:T(8,128)}) async-done(((f32[1,1024,8]{1,2,0:T(8,128)}, f32[1,1024,8]{1,2,0:T(8,128)}), (f32[1,1024,8]{1,2,0:T(8,128)}, f32[1,1024,8]{1,2,0:T(8,128)})) %all-reduce.9.cloned.1.call-update) | async-done | bytes 65552 | tf_op jit(solution)/shard_map/psum | solution.py:12
  234.1 1.0 fusion.32
  235.1 1.0 fusion.33
  236.2 0.7 custom-call.8
  236.9 0.6 compare_reduce_fusion.1
  237.6 0.6 fusion.54
  238.2 0.6 custom-call.9
  238.9 1.0 fusion.36
  239.9 0.7 custom-call.10
  240.7 0.6 compare_reduce_fusion
  241.3 0.6 fusion.55
  242.0 0.6 custom-call.11
  242.6 1.1 fusion.34
  243.7 4.3 fusion.29
  248.1 3.8 fusion.26
  251.9 249.1 %all-reduce = (f32[1,896,8]{1,2,0:T(8,128)S(1)}, f32[1,896,8]{1,2,0:T(8,128)S(1)}) all-reduce(f32[1,896,8]{1,2,0:T(8,128)S(1)} %fusion.29, f32[1,896,8]{1,2,0:T(8,128)S(1)} %fusion.26), channel_id=1, replica_groups=mesh['dp'=64,'outer'=4] {'dp'}, use_global_device_ids=true, to_apply=%region_8.11 | all-reduce | flops 14336 | bytes 114688 | tf_op jit(solution)/shard_map/psum | solution.py:16
  501.0 16.6 %all-reduce.2 = (f32[1,896,8]{1,2,0:T(8,128)S(1)}, f32[1,896,8]{1,2,0:T(8,128)S(1)}) all-reduce(f32[1,896,8]{1,2,0:T(8,128)S(1)} %get-tuple-element.4, f32[1,896,8]{1,2,0:T(8,128)S(1)} %get-tuple-element.5), channel_id=1, replica_groups=mesh['dp'=64,'outer'=4] {'outer'}, use_global_device_ids=true, to_apply=%region_9.12 | all-reduce | flops 14336 | bytes 114688 | tf_op jit(solution)/shard_map/psum | solution.py:17
  517.6 5.0 fusion.10
  522.7 4.7 fusion.11
  527.3 0.6 pad_maximum_fusion
  528.0 2.2 maximum_bitcast_fusion
  (19 shorter events, 0.4 us)
Async XLA Ops:
  7.2 6.4 %copy-start.3 = (f32[2,896,8]{1,2,0:T(8,128)S(1)}, f32[2,896,8]{1,2,0:T(8,128)}, u32[]{:S(2)}) copy-start(f32[2,896,8]{1,2,0:T(8,128)} %param.8) | copy-start | bytes 172036
  7.2 181.4 %all-reduce.7.cloned.1.call-start = ((), (), s32[]{:S(2)}) async-start(), calls=%async_computation | async-start | bytes 131072 | tf_op jit(solution)/shard_map/psum | solution.py:11
  7.2 6.3 %copy-start = (bf16[1,1,2,1024,896]{4,3,2,1,0:T(8,128)(2,1)S(1)}, bf16[1,1,2,1024,896]{4,3,2,1,0:T(8,128)(2,1)}, u32[]{:S(2)}) copy-start(bf16[1,1,2,1024,896]{4,3,2,1,0:T(8,128)(2,1)} %param.7) | copy-start | bytes 11010052
  19.2 214.9 %all-reduce.9.cloned.1.call-start = ((), (), s32[]{:S(2)}) async-start(), calls=%async_computation.1 | async-start | bytes 131072 | tf_op jit(solution)/shard_map/psum | solution.py:12
  242.6 5.5 %copy-start.1 = (bf16[1,1,2,1024,896]{4,3,2,1,0:T(8,128)(2,1)S(1)}, bf16[1,1,2,1024,896]{4,3,2,1,0:T(8,128)(2,1)}, u32[]{:S(2)}) copy-start(bf16[1,1,2,1024,896]{4,3,2,1,0:T(8,128)(2,1)} %param.7) | copy-start | bytes 11010052
  517.6 5.1 copy-start.2
Sparse Core Ops, SparseCore 0:
  19.3 169.2 all-reduce.6
  190.9 43.0 all-reduce.8
where the time goes:
time: 537 us
  blocking collectives  266 us (50%)
  waiting for transfers between devices  215 us (40%)
  matrix products  33.9 us (6%)
  between operations  14.2 us (3%)
  other arithmetic  8.2 us (2%)
    psum x1, blocking collectives, sum_right(): group_sum = lax.psum(partial_right, 'dp')  249 us
    psum x1, waiting for transfers between devices, sum_left(): group_sum = lax.psum(partial_left, 'dp')  169 us
    psum x1, waiting for transfers between devices, sum_left(): return lax.psum(group_sum, 'outer')  45.5 us
    psum x1, blocking collectives, sum_right(): return lax.psum(group_sum, 'outer')  16.6 us
    dot_general x2, matrix products, compress(): jnp.einsum('krc,kcs->krs', merged, basis_part, precision=HIGHEST)  11.9 us
  transfers between devices with their start and end apart: 2, of which 2 were waited for; matrix products, arithmetic and copies ran while one was open for 0% of the time, Pallas kernels for 0%

commit v1 on v0

--- a/solution.py
+++ b/solution.py
@@ -9,7 +9,7 @@
 
 def sum_left(partial_left):
     group_sum = lax.psum(partial_left, "dp")
-    return lax.psum(group_sum, "outer")
+    return jnp.sum(lax.all_gather(group_sum, "outer"), axis=0)
 
 
 def sum_right(partial_right):

time: 537 us -> 512 us (0.953)
  waiting for transfers between devices: 215 us -> 169 us
  blocking collectives: 266 us -> 288 us
    psum x1 -> x0, waiting for transfers between devices: 45.5 us -> none  [sum_left(): return lax.psum(group_sum, 'outer')]
    all_gather x0 -> x2, blocking collectives: none -> 24.7 us  [sum_left(): return jnp.sum(lax.all_gather(group_sum, 'outer'), axis=0)]
  transfers between devices with their start and end apart: 2 -> 1, of which waited for: 2 -> 1; matrix products, arithmetic and copies ran while one was open for 0% -> 0% of each run, Pallas kernels for 0% -> 0%
where the time goes in v1:
time: 512 us; the launch traced here: 511 us
  blocking collectives  288 us (56%)
  waiting for transfers between devices  169 us (33%)
  matrix products  31.1 us (6%)
  between operations  14.2 us (3%)
  other arithmetic  8.24 us (2%)
    psum x1, blocking collectives, sum_right(): group_sum = lax.psum(partial_right, 'dp')  246 us
    psum x1, waiting for transfers between devices, sum_left(): group_sum = lax.psum(partial_left, 'dp')  169 us
    all_gather x2, blocking collectives, sum_left(): return jnp.sum(lax.all_gather(group_sum, 'outer'), axis=0)  24.7 us
    psum x1, blocking collectives, sum_right(): return lax.psum(group_sum, 'outer')  17.2 us
    dot_general x2, matrix products, compress(): jnp.einsum('krc,kcs->krs', merged, basis_part, precision=HIGHEST)  11.9 us
  transfers between devices with their start and end apart: 1, of which 1 were waited for; matrix products, arithmetic and copies ran while one was open for 0% of the time, Pallas kernels for 0%

profile of v1, /device:TPU:0, one launch (start us, length us, event | category | flops | bytes accessed | tf_op | source)
XLA Modules:
  0.0 511.3 jit_solution(11911221716146827499)
XLA Ops:
  7.2 6.3 %fusion.23 = f32[1,1,1024,8]{2,3,1,0:T(8,128)} fusion(bf16[1,1,2,1024,896]{4,3,2,1,0:T(8,128)(2,1)} %param.7, bf16[1,1,2,1024,896]{4,3,2,1,0:T(8,128)(2,1)} %param.6, f32[2,896,8]{1,2,0:T(8,128)} %param.8), kind=kOutput, calls=%fused_computation.26 | convolution fusion | flops 90832896 | bytes 3731456 | tf_op jit(solution)/shard_map/krc,kcs->krs/dot_general | solution.py:29
  13.5 5.6 %fusion.20 = f32[1,1,1024,8]{2,3,1,0:T(8,128)} fusion(bf16[1,1,2,1024,896]{4,3,2,1,0:T(8,128)(2,1)S(1)} %copy-done, bf16[1,1,2,1024,896]{4,3,2,1,0:T(8,128)(2,1)} %param.6, f32[2,896,8]{1,2,0:T(8,128)S(1)} %copy-done.3), kind=kOutput, calls=%fused_computation.25 | convolution fusion | flops 90832896 | bytes 3731456 | tf_op jit(solution)/shard_map/krc,kcs->krs/dot_general | solution.py:29
  19.2 169.4 %all-reduce.5.cloned.1.call-done = (f32[1,1,1024,8]{2,3,1,0:T(8,128)}, f32[1,1,1024,8]{2,3,1,0:T(8,128)}) async-done(((f32[1,1,1024,8]{2,3,1,0:T(8,128)}, f32[1,1,1024,8]{2,3,1,0:T(8,128)}), (f32[1,1,1024,8]{2,3,1,0:T(8,128)}, f32[1,1,1024,8]{2,3,1,0:T(8,128)})) %all-reduce.5.cloned.1.call-update) | async-done | bytes 65552 | tf_op jit(solution)/shard_map/psum | solution.py:11
  188.5 12.7 %all_gather.15 = f32[4,1,1024,8]{2,3,1,0:T(8,128)S(1)} all-gather(f32[1,1,1024,8]{2,3,1,0:T(8,128)} %get-tuple-element.6), channel_id=1, replica_groups=mesh['dp'=64,'outer'=4] {'outer'}, dimensions={0}, use_global_device_ids=true | all-gather | bytes 163840 | tf_op jit(solution)/shard_map/all_gather | solution.py:12
  201.5 0.7 custom-call.10
  202.2 0.6 compare_reduce_fusion
  202.9 0.6 fusion.53
  203.5 0.6 custom-call.11
  204.2 0.2 fusion.34
  204.4 4.3 fusion.29
  208.8 12.0 %all_gather.13 = f32[4,1,1024,8]{2,3,1,0:T(8,128)S(1)} all-gather(f32[1,1,1024,8]{2,3,1,0:T(8,128)S(1)} %copy-done.2), channel_id=1, replica_groups=mesh['dp'=64,'outer'=4] {'outer'}, dimensions={0}, use_global_device_ids=true | all-gather | bytes 163840 | tf_op jit(solution)/shard_map/all_gather | solution.py:12
  220.8 0.2 fusion.33
  221.0 0.7 custom-call.8
  221.8 0.6 compare_reduce_fusion.1
  222.4 0.6 fusion.52
  223.1 0.6 custom-call.9
  223.7 0.2 fusion.36
  223.9 4.3 fusion.26
  228.3 246.4 %all-reduce = (f32[1,896,8]{1,2,0:T(8,128)S(1)}, f32[1,896,8]{1,2,0:T(8,128)S(1)}) all-reduce(f32[1,896,8]{1,2,0:T(8,128)S(1)} %fusion.29, f32[1,896,8]{1,2,0:T(8,128)S(1)} %fusion.26), channel_id=1, replica_groups=mesh['dp'=64,'outer'=4] {'dp'}, use_global_device_ids=true, to_apply=%region_8.11 | all-reduce | flops 14336 | bytes 114688 | tf_op jit(solution)/shard_map/psum | solution.py:16
  474.7 17.2 %all-reduce.2 = (f32[1,896,8]{1,2,0:T(8,128)S(1)}, f32[1,896,8]{1,2,0:T(8,128)S(1)}) all-reduce(f32[1,896,8]{1,2,0:T(8,128)S(1)} %get-tuple-element.4, f32[1,896,8]{1,2,0:T(8,128)S(1)} %get-tuple-element.5), channel_id=1, replica_groups=mesh['dp'=64,'outer'=4] {'outer'}, use_global_device_ids=true, to_apply=%region_9.12 | all-reduce | flops 14336 | bytes 114688 | tf_op jit(solution)/shard_map/psum | solution.py:17
  491.9 5.0 fusion.10
  496.9 4.7 fusion.11
  501.6 0.6 pad_maximum_fusion
  502.2 2.2 maximum_bitcast_fusion
  (20 shorter events, 0.6 us)
Async XLA Ops:
  7.2 6.4 %copy-start.3 = (f32[2,896,8]{1,2,0:T(8,128)S(1)}, f32[2,896,8]{1,2,0:T(8,128)}, u32[]{:S(2)}) copy-start(f32[2,896,8]{1,2,0:T(8,128)} %param.8) | copy-start | bytes 172036
  7.2 181.4 %all-reduce.5.cloned.1.call-start = ((), (), s32[]{:S(2)}) async-start(), calls=%async_computation | async-start | bytes 131072 | tf_op jit(solution)/shard_map/psum | solution.py:11
  7.2 6.3 %copy-start = (bf16[1,1,2,1024,896]{4,3,2,1,0:T(8,128)(2,1)S(1)}, bf16[1,1,2,1024,896]{4,3,2,1,0:T(8,128)(2,1)}, u32[]{:S(2)}) copy-start(bf16[1,1,2,1024,896]{4,3,2,1,0:T(8,128)(2,1)} %param.7) | copy-start | bytes 11010052
  188.5 20.2 %copy-start.2 = (f32[1,1,1024,8]{2,3,1,0:T(8,128)S(1)}, f32[1,1,1024,8]{2,3,1,0:T(8,128)}, u32[]{:S(2)}) copy-start(f32[1,1,1024,8]{2,3,1,0:T(8,128)} %get-tuple-element.7) | copy-start | bytes 98308
  491.9 5.1 copy-start.1
Sparse Core Ops, SparseCore 0:
  19.3 169.2 all-reduce.4
